TPU v7x, 32 devices: a whole 2x2x4 slice. The times are simulated.
32 devices in a mesh: parts: 2 (over x), tensor: 16 (over z, y, core).
Axes of the slice: x: 2, y: 2, z: 4, core: 2. Of those that a mesh axis runs over, the one named last changes fastest.
Arguments:
- tokens: bfloat16 [128, 6144], P(('parts', 'tensor')), parts along dimension 0, may hold values from -6 to 6
- route_ids: int32 [128, 2], P(('parts', 'tensor')), parts along dimension 0, may hold values from 0 to 3, all different within a row; in each aligned block of 4 rows (0 to 3, 4 to 7, ...) at most 3 rows name the same one
- gate_values: bfloat16 [128, 2], P(('parts', 'tensor')), parts along dimension 0, may hold values from 0.099609375 to 0.8984375
- w_gate: bfloat16 [6144, 32768], P(None, 'tensor'), may hold values from -0.078125 to 0.078125
- w_up: bfloat16 [6144, 32768], P(None, 'tensor'), may hold values from -0.078125 to 0.078125
- w_down: bfloat16 [32768, 6144], P('tensor'), may hold values from -0.0625 to 0.0625
Outputs:
- mixed: bfloat16 [128, 6144], P(('parts', 'tensor')), parts along dimension 0
There are 2 independent parts, one for each index of `parts`. A program takes and returns all parts, laid end to end along the dimension named above; an argument that names none is the same for every part. Nothing has to cross between parts.
Inputs may be any that keep to these rules, and one draw needn't show every extreme that they name: `route_ids`: each row names two different experts; the rows of one device name any one expert at most 3 times, and that bound is reached in every draw.
All inputs are finite; a program needn't handle non-finite values.
Results may differ from a plain program's by a relative error of at most 0.0049.
Values may be sent and summed in bfloat16 or wider, within the bound.
A program may use at most 192 MiB of HBM per device.

v0:
```python
import jax
import jax.numpy as jnp
from jax import lax
from jax.sharding import PartitionSpec as P

EXPERTS = 4
BLOCK = 128
MOST = 3


def partner(shard, axis, stride):
    return lax.ppermute(shard, axis, [(i, i ^ 1 << stride) for i in range(lax.axis_size(axis))])


def from_behind(block, axis, distance):
    devices = range(lax.axis_size(axis))
    route = [((i - distance) % len(devices), i) for i in devices]
    return lax.ppermute(block, axis, route)


def expert_blocks(compact, occupied, w_gate, w_up, w_down):
    capacity = compact.shape[0]

    def block_step(block_index, buffer):

        def block_work(inner):
            block_rows = lax.dynamic_slice_in_dim(compact, block_index * BLOCK, BLOCK, 0)
            gate_proj = jnp.dot(block_rows, w_gate, preferred_element_type=jnp.float32)
            up_proj = jnp.dot(block_rows, w_up, preferred_element_type=jnp.float32)
            hidden = (jax.nn.silu(gate_proj) * up_proj).astype(jnp.bfloat16)
            output_rows = jnp.dot(hidden, w_down, preferred_element_type=jnp.float32)
            return lax.dynamic_update_slice_in_dim(inner, output_rows, block_index * BLOCK, 0)

        def block_skip(inner):
            return inner

        return lax.cond(block_index * BLOCK < occupied, block_work, block_skip, buffer)

    start_buffer = jnp.zeros((capacity, w_down.shape[1]), jnp.float32)
    return lax.fori_loop(0, capacity // BLOCK, block_step, start_buffer)


def per_device(tokens, route_ids, gate_values, w_gate, w_up, w_down):
    tensor_size = lax.axis_size("tensor")
    group_size = tensor_size // EXPERTS
    my_index = lax.axis_index("tensor")
    expert = my_index // group_size
    local_rows = tokens.shape[0]
    width = tokens.shape[1]
    total_rows = local_rows * tensor_size
    capacity = (total_rows + BLOCK - 1) // BLOCK * BLOCK
    all_routes = lax.all_gather(route_ids, "tensor", axis=0, tiled=True)
    routed = all_routes == expert
    selected = jnp.any(routed, axis=1).astype(jnp.int32)
    occupied = jnp.sum(selected)
    expert_list = jnp.arange(EXPERTS, dtype=jnp.int32)
    local_hits = jnp.any(route_ids[:, :, None] == expert_list[None, None, :], axis=1).astype(
        jnp.int32
    )
    local_place = jnp.cumsum(local_hits, axis=0) - 1
    target = jnp.where(local_hits > 0, local_place, MOST)
    row_numbers = jnp.broadcast_to(jnp.arange(local_rows, dtype=jnp.int32)[:, None], target.shape)
    send_rows = (
        jnp.full((EXPERTS, MOST), local_rows, jnp.int32)
        .at[jnp.broadcast_to(expert_list[None, :], target.shape), target]
        .set(row_numbers, mode="drop")
    )
    outgoing = jnp.take(tokens, send_rows.reshape(-1), axis=0, mode="fill", fill_value=0)
    outgoing = outgoing.reshape(EXPERTS, 1, MOST, width)
    outgoing = jnp.broadcast_to(outgoing, (EXPERTS, group_size, MOST, width)).reshape(
        tensor_size * MOST, width
    )
    received = lax.all_to_all(outgoing, "tensor", split_axis=0, concat_axis=0, tiled=True)
    per_source = jnp.sum(selected.reshape(tensor_size, local_rows), axis=1)
    source_start = jnp.cumsum(per_source) - per_source
    place = jnp.arange(MOST, dtype=jnp.int32)
    landing = jnp.where(
        place[None, :] < per_source[:, None], source_start[:, None] + place[None, :], capacity
    )
    inverse = (
        jnp.full((capacity,), tensor_size * MOST, jnp.int32)
        .at[landing.reshape(-1)]
        .set(jnp.arange(tensor_size * MOST, dtype=jnp.int32), mode="drop")
    )
    compact = jnp.take(received, inverse, axis=0, mode="fill", fill_value=0)
    partial_value = expert_blocks(compact, occupied, w_gate, w_up, w_down)
    returning = jnp.take(partial_value, landing.reshape(-1), axis=0, mode="fill", fill_value=0)
    levels = group_size.bit_length() - 1
    buffer = jnp.transpose(returning.reshape(EXPERTS, group_size, MOST, width), (1, 0, 2, 3))
    for bit in range(levels - 1, -1, -1):
        half = buffer.shape[0] // 2
        lower = buffer[:half]
        upper = buffer[half:]
        high_side = my_index >> bit & 1 == 1
        keep = jnp.where(high_side, upper, lower)
        give = jnp.where(high_side, lower, upper)
        buffer = keep + partner(give, "tensor", bit)
    reduced = buffer[0]
    collected = jnp.zeros((EXPERTS, MOST, width), jnp.float32)
    own_piece = lax.dynamic_index_in_dim(reduced, expert, 0, keepdims=True)
    collected = lax.dynamic_update_slice_in_dim(collected, own_piece, expert, 0)
    for offset in range(1, EXPERTS):
        piece = lax.dynamic_index_in_dim(reduced, (expert + offset) % EXPERTS, 0, keepdims=True)
        arrived_piece = from_behind(piece, "tensor", offset * group_size)
        source_expert = (expert - offset + EXPERTS) % EXPERTS
        collected = lax.dynamic_update_slice_in_dim(collected, arrived_piece, source_expert, 0)
    per_expert = collected.reshape(EXPERTS * MOST, width)
    mixed_rows = jnp.zeros((local_rows, width), jnp.float32)
    for column in range(2):
        chosen = route_ids[:, column]
        chosen_place = jnp.take_along_axis(local_place, chosen[:, None], axis=1)[:, 0]
        picked = jnp.take(per_expert, chosen * MOST + chosen_place, axis=0)
        mixed_rows = mixed_rows + gate_values[:, column].astype(jnp.float32)[:, None] * picked
    return mixed_rows.astype(jnp.bfloat16)


def solution(mesh):
    in_specs = (
        P(("parts", "tensor"), None),
        P(("parts", "tensor"), None),
        P(("parts", "tensor"), None),
        P(None, "tensor"),
        P(None, "tensor"),
        P("tensor", None),
    )
    out_specs = P(("parts", "tensor"), None)
    return jax.shard_map(
        per_device, mesh=mesh, in_specs=in_specs, out_specs=out_specs, check_vma=False
    )
```

profile of v0, /device:TPU:0, one launch (start us, length us, event | category | flops | bytes accessed | tf_op | source)
XLA Modules:
  0.0 114.0 jit_solution(6621758022598223172)
XLA Ops:
  0.0 0.8 fusion.15
  1.0 1.3 %scatter_fusion = s32[4,3]{1,0:T(4,128)S(1)} fusion(s32[4,3]{1,0:T(4,128)S(1)} %broadcast.232, s32[16]{0:T(128)S(1)} %reshape.325, s32[16]{0:T(128)S(1)} %reshape.327), kind=kCustom, calls=%fused_computation.8 | custom fusion | bytes 320 | tf_op jit(solution)/shard_map/scatter | solution.py:66
  3.3 1.2 %broadcast_in_dim.118 = bf16[4,4,3,6144]{3,2,1,0:T(4,128)(2,1)} broadcast(bf16[4,3,6144]{2,1,0:T(4,128)(2,1)S(1)} %broadcast_select_fusion.4), dimensions={0,2,3} | broadcast | bytes 737280 | tf_op jit(solution)/shard_map/broadcast_in_dim | solution.py:70
  4.5 7.4 %all-to-all-start = ((bf16[16,3,6144]{2,1,0:T(4,128)(2,1)}), bf16[16,3,6144]{2,1,0:T(4,128)(2,1)S(1)}, u32[]{:S(2)}, u32[]{:S(2)}) async-start(bf16[16,3,6144]{2,1,0:T(4,128)(2,1)} %bitcast.11), calls=%async_computation | async-start | bytes 1572864 | tf_op jit(solution)/shard_map/all_to_all | solution.py:73
  11.9 29.2 %all-gather = s32[16,4,2]{1,2,0:T(2,128)S(1)} all-gather(s32[1,4,2]{1,2,0:T(2,128)S(1)} %bitcast.60), channel_id=1, replica_groups=mesh['parts'=2,'tensor'=16] {'tensor'}, dimensions={0}, use_global_device_ids=true | all-gather | bytes 544 | tf_op jit(solution)/shard_map/all_gather | solution.py:52
  41.2 0.6 convert_reduce_fusion
  43.1 0.7 scatter_custom_fusion
  44.0 33.9 %conditional.1 = (f32[128,6144]{1,0:T(8,128)S(1)}) conditional(s32[]{:T(128)} %convert_element_type.40, () %tuple.25, (s32[128]{0:T(128)S(1)}, bf16[16,3,6144]{2,1,0:T(4,128)(2,1)S(1)}, bf16[6144,2048]{1,0:T(8,128)(2,1)}, bf16[6144,2048]{1,0:T(8,128)(2,1)}, bf16[2048,6144]{1,0:T(8,128)(2,1)}) %tuple.26), branch_computations={%region_8.9_spmd, %region_9.10_spmd} | conditional | flops 9666824192 | bytes 94509992 | solution.py:37
  44.6 1.5 %gather_fusion = bf16[128,6144]{1,0:T(8,128)(2,1)S(1)} fusion(bf16[48,6144]{1,0:T(8,128)(2,1)S(1)} %all_to_all.2, s32[1024]{0:T(1024)S(1)} %pad_clamp_fusion), kind=kCustom, calls=%fused_computation | custom fusion | bytes 3146240 | tf_op jit(solution)/shard_map/jit(_take)/gather | solution.py:85
  46.1 13.1 %fusion.7 = f32[128,2048]{1,0:T(8,128)} fusion(bf16[6144,2048]{1,0:T(8,128)(2,1)} %get-tuple-element.129, bf16[128,6144]{1,0:T(8,128)(2,1)S(1)} %gather_fusion, pred[128]{0:T(512)(128)(4,1)S(1)} %compare_and_fusion), kind=kOutput, calls=%fused_computation.18 | convolution fusion | flops 3222011904 | bytes 27787392 | tf_op jit(solution)/shard_map/while/body/eval_jaxpr/cond/branch_1_fun/dot_general | solution.py:28
  59.3 18.4 %fusion.1 = f32[128,6144]{1,0:T(8,128)S(1)} fusion(bf16[2048,6144]{1,0:T(8,128)(2,1)} %get-tuple-element.131, bf16[6144,2048]{1,0:T(8,128)(2,1)} %get-tuple-element.130, f32[128,2048]{1,0:T(8,128)} %fusion.7, bf16[128,6144]{1,0:T(8,128)(2,1)} %copy-done.2, pred[128]{0:T(512)(128)(4,1)S(1)} %compare_and_fusion), kind=kOutput, calls=%fused_computation.11 | convolution fusion | flops 6444810240 | bytes 56098944 | tf_op jit(solution)/shard_map/while/body/eval_jaxpr/cond/branch_1_fun/dot_general | solution.py:31
  77.9 1.9 %gather_fusion.2 = f32[48,6144]{1,0:T(8,128)} fusion(f32[128,6144]{1,0:T(8,128)S(1)} %get-tuple-element.151, s32[1024]{0:T(1024)S(1)} %pad_clamp_fusion.3), kind=kCustom, calls=%fused_computation.6 | custom fusion | bytes 2359488 | tf_op jit(solution)/shard_map/jit(_take)/gather | solution.py:87
  79.8 1.6 %gather.28 = f32[4,4,3,6144]{3,2,1,0:T(4,128)S(1)} reshape(f32[48,6144]{1,0:T(8,128)} %gather_fusion.2) | data formatting | bytes 2359296 | tf_op jit(solution)/shard_map/jit(_take)/gather | solution.py:87
  82.5 1.9 %collective-permute-start = (f32[2,4,3,6144]{3,1,2,0:T(4,128)S(1)}, f32[2,4,3,6144]{3,1,2,0:T(4,128)S(1)}, u32[]{:S(2)}, u32[]{:S(2)}) collective-permute-start(f32[2,4,3,6144]{3,1,2,0:T(4,128)S(1)} %copy.28), channel_id=1, source_target_pairs={{0,2},{1,3},{2,0},{3,1},{4,6},{5,7},{6,4},{7,5},{8,10},{9,11},{10,... | collective-permute-start | bytes 1769480 | tf_op jit(solution)/shard_map/ppermute | solution.py:12
  84.5 0.6 gather_fusion.3
  85.1 0.6 gather_fusion.5
  85.8 12.4 %collective-permute-done = f32[2,4,3,6144]{3,1,2,0:T(4,128)S(1)} collective-permute-done((f32[2,4,3,6144]{3,1,2,0:T(4,128)S(1)}, f32[2,4,3,6144]{3,1,2,0:T(4,128)S(1)}, u32[]{:S(2)}, u32[]{:S(2)}) %collective-permute-start) | collective-permute-done | bytes 589856 | tf_op jit(solution)/shard_map/ppermute | solution.py:12
  99.0 1.7 %collective-permute-done.1 = f32[1,4,3,6144]{3,2,0,1:T(4,128)S(1)} collective-permute-done((f32[1,4,3,6144]{3,2,0,1:T(4,128)S(1)}, f32[1,4,3,6144]{3,2,0,1:T(4,128)S(1)}, u32[]{:S(2)}, u32[]{:S(2)}) %collective-permute-start.1) | collective-permute-done | bytes 294944 | tf_op jit(solution)/shard_map/ppermute | solution.py:12
  100.9 2.2 %collective-permute-start.2 = (f32[1,3,6144]{2,1,0:T(4,128)S(1)}, f32[1,3,6144]{2,1,0:T(4,128)S(1)}, u32[]{:S(2)}, u32[]{:S(2)}) collective-permute-start(f32[1,3,6144]{2,1,0:T(4,128)S(1)} %get-tuple-element.140), channel_id=1, source_target_pairs={{12,0},{13,1},{14,2},{15,3},{0,4},{1,5},{2,6},{3,7},{4,8},{5,9},{6... | collective-permute-start | bytes 221192 | tf_op jit(solution)/shard_map/ppermute | solution.py:18
  103.0 1.5 %collective-permute-start.3 = (f32[1,3,6144]{2,1,0:T(4,128)S(1)}, f32[1,3,6144]{2,1,0:T(4,128)S(1)}, u32[]{:S(2)}, u32[]{:S(2)}) collective-permute-start(f32[1,3,6144]{2,1,0:T(4,128)S(1)} %get-tuple-element.139), channel_id=1, source_target_pairs={{8,0},{9,1},{10,2},{11,3},{12,4},{13,5},{14,6},{15,7},{0,8},{1,9},... | collective-permute-start | bytes 221192 | tf_op jit(solution)/shard_map/ppermute | solution.py:18
  104.5 2.4 %collective-permute-start.4 = (f32[1,3,6144]{2,1,0:T(4,128)S(1)}, f32[1,3,6144]{2,1,0:T(4,128)S(1)}, u32[]{:S(2)}, u32[]{:S(2)}) collective-permute-start(f32[1,3,6144]{2,1,0:T(4,128)S(1)} %get-tuple-element.138), channel_id=1, source_target_pairs={{4,0},{5,1},{6,2},{7,3},{8,4},{9,5},{10,6},{11,7},{12,8},{13,9},{1... | collective-permute-start | bytes 221192 | tf_op jit(solution)/shard_map/ppermute | solution.py:18
  107.0 1.0 collective-permute-done.2
  107.9 3.9 %collective-permute-done.3 = f32[1,3,6144]{2,1,0:T(4,128)S(1)} collective-permute-done((f32[1,3,6144]{2,1,0:T(4,128)S(1)}, f32[1,3,6144]{2,1,0:T(4,128)S(1)}, u32[]{:S(2)}, u32[]{:S(2)}) %collective-permute-start.3) | collective-permute-done | bytes 73760 | tf_op jit(solution)/shard_map/ppermute | solution.py:18
  113.3 0.7 fusion.14
  (70 shorter events, 6.2 us)
Async XLA Ops:
  0.0 2.4 %copy-start = (bf16[4,6144]{1,0:T(4,128)(2,1)S(1)}, bf16[4,6144]{1,0:T(4,128)(2,1)}, u32[]{:S(2)}) copy-start(bf16[4,6144]{1,0:T(4,128)(2,1)} %param.12) | copy-start | bytes 147460
  3.2 8.8 %copy-start.3 = (s32[4,2]{0,1:T(2,128)S(1)}, s32[4,2]{0,1:T(2,128)}, u32[]{:S(2)}) copy-start(s32[4,2]{0,1:T(2,128)} %param.13) | copy-start | bytes 100
  4.5 39.5 %all-to-all-start = ((bf16[16,3,6144]{2,1,0:T(4,128)(2,1)}), bf16[16,3,6144]{2,1,0:T(4,128)(2,1)S(1)}, u32[]{:S(2)}, u32[]{:S(2)}) async-start(bf16[16,3,6144]{2,1,0:T(4,128)(2,1)} %bitcast.11), calls=%async_computation | async-start | bytes 1572864 | tf_op jit(solution)/shard_map/all_to_all | solution.py:73
  46.1 13.2 %copy-start.2 = (bf16[128,6144]{1,0:T(8,128)(2,1)}, bf16[128,6144]{1,0:T(8,128)(2,1)S(1)}, u32[]{:S(2)}) copy-start(bf16[128,6144]{1,0:T(8,128)(2,1)S(1)} %gather_fusion) | copy-start | bytes 4718596 | tf_op jit(solution)/shard_map/while/body/eval_jaxpr/cond
  82.5 15.7 %collective-permute-start = (f32[2,4,3,6144]{3,1,2,0:T(4,128)S(1)}, f32[2,4,3,6144]{3,1,2,0:T(4,128)S(1)}, u32[]{:S(2)}, u32[]{:S(2)}) collective-permute-start(f32[2,4,3,6144]{3,1,2,0:T(4,128)S(1)} %copy.28), channel_id=1, source_target_pairs={{0,2},{1,3},{2,0},{3,1},{4,6},{5,7},{6,4},{7,5},{8,10},{9,11},{10,... | collective-permute-start | bytes 1769480 | tf_op jit(solution)/shard_map/ppermute | solution.py:12
  85.8 13.2 %copy-start.4 = (bf16[4,2]{0,1:T(2,128)(2,1)S(1)}, bf16[4,2]{0,1:T(2,128)(2,1)}, u32[]{:S(2)}) copy-start(bf16[4,2]{0,1:T(2,128)(2,1)} %param.14) | copy-start | bytes 52
  98.9 1.8 %collective-permute-start.1 = (f32[1,4,3,6144]{3,2,0,1:T(4,128)S(1)}, f32[1,4,3,6144]{3,2,0,1:T(4,128)S(1)}, u32[]{:S(2)}, u32[]{:S(2)}) collective-permute-start(f32[1,4,3,6144]{3,2,0,1:T(4,128)S(1)} %slice_select_fusion.1), channel_id=1, source_target_pairs={{0,1},{1,0},{2,3},{3,2},{4,5},{5,4},{6,7},{7,6},{8,9},{9,8},{10,11... | collective-permute-start | bytes 884744 | tf_op jit(solution)/shard_map/ppermute | solution.py:12
  100.9 7.1 %collective-permute-start.2 = (f32[1,3,6144]{2,1,0:T(4,128)S(1)}, f32[1,3,6144]{2,1,0:T(4,128)S(1)}, u32[]{:S(2)}, u32[]{:S(2)}) collective-permute-start(f32[1,3,6144]{2,1,0:T(4,128)S(1)} %get-tuple-element.140), channel_id=1, source_target_pairs={{12,0},{13,1},{14,2},{15,3},{0,4},{1,5},{2,6},{3,7},{4,8},{5,9},{6... | collective-permute-start | bytes 221192 | tf_op jit(solution)/shard_map/ppermute | solution.py:18
  103.0 8.8 %collective-permute-start.3 = (f32[1,3,6144]{2,1,0:T(4,128)S(1)}, f32[1,3,6144]{2,1,0:T(4,128)S(1)}, u32[]{:S(2)}, u32[]{:S(2)}) collective-permute-start(f32[1,3,6144]{2,1,0:T(4,128)S(1)} %get-tuple-element.139), channel_id=1, source_target_pairs={{8,0},{9,1},{10,2},{11,3},{12,4},{13,5},{14,6},{15,7},{0,8},{1,9},... | collective-permute-start | bytes 221192 | tf_op jit(solution)/shard_map/ppermute | solution.py:18
  104.5 7.4 %collective-permute-start.4 = (f32[1,3,6144]{2,1,0:T(4,128)S(1)}, f32[1,3,6144]{2,1,0:T(4,128)S(1)}, u32[]{:S(2)}, u32[]{:S(2)}) collective-permute-start(f32[1,3,6144]{2,1,0:T(4,128)S(1)} %get-tuple-element.138), channel_id=1, source_target_pairs={{4,0},{5,1},{6,2},{7,3},{8,4},{9,5},{10,6},{11,7},{12,8},{13,9},{1... | collective-permute-start | bytes 221192 | tf_op jit(solution)/shard_map/ppermute | solution.py:18
  107.9 6.1 %copy-start.1 = (bf16[4,6144]{1,0:T(4,128)(2,1)S(1)}, bf16[4,6144]{1,0:T(4,128)(2,1)}, u32[]{:S(2)}) copy-start(bf16[4,6144]{1,0:T(4,128)(2,1)} %param.12) | copy-start | bytes 147460
where the time goes:
time: 114 us
  matrix products  31.6 us (28%)
  blocking collectives  29.2 us (26%)
  waiting for transfers between devices  18.9 us (17%)
  starting transfers between devices  15.3 us (13%)
  local copies, waits for them, and re-layouts  13.4 us (12%)
  other arithmetic  4.3 us (4%)
    all_gather x1, blocking collectives, per_device(): all_routes = lax.all_gather(route_ids, 'tensor', axis=0, tiled=True)  29.2 us
    dot_general x1, matrix products, block_work(): output_rows = jnp.dot(hidden, w_down, preferred_element_type=jnp.float32)  18.4 us
    ppermute x2, waiting for transfers between devices, partner(): lax.ppermute(shard, axis, [(i, i ^ 1 << stride) for i in range(lax.axis_s...  14.1 us
    dot_general x1, matrix products, block_work(): gate_proj = jnp.dot(block_rows, w_gate, preferred_element_type=jnp.float32)  13.1 us
    all_to_all x1, starting transfers between devices, per_device(): lax.all_to_all(outgoing, 'tensor', split_axis=0, concat_axis=0, tiled=True)  7.39 us
    ppermute x3, starting transfers between devices, from_behind(): return lax.ppermute(block, axis, route)  5.99 us
    ppermute x3, waiting for transfers between devices, from_behind(): return lax.ppermute(block, axis, route)  4.88 us
    gather x2, local copies, waits for them, and re-layouts, per_device(): jnp.take(partial_value, landing.reshape(-1), axis=0, mode='fill', fill_va...  3.5 us
  transfers between devices with their start and end apart: 6, of which 4 were waited for; matrix products, arithmetic and copies ran while one was open for 3% of the time, Pallas kernels for 0%

commit v1 on v0

--- a/solution.py
+++ b/solution.py
@@ -1,11 +1,312 @@
+import functools
+
 import jax
 import jax.numpy as jnp
 from jax import lax
+from jax.experimental import pallas as pl
+from jax.experimental.pallas import tpu as pltpu
 from jax.sharding import PartitionSpec as P
 
 EXPERTS = 4
 BLOCK = 128
 MOST = 3
+DEVICES = 16
+ROWS_DEV = 4
+FOLD = 4
+K_CHUNKS = 8
+GU_SLOTS = 4
+D_EARLY = 4
+CHUNK = 512
+SKEW = 2
+LANES = 128
+MESH = pl.DeviceIdType.MESH
+
+
+def spread(first, second, upper):
+    low = lax.broadcasted_iota(jnp.int32, first.shape, 0) < 4
+    if upper:
+        return jnp.where(low, pltpu.roll(first, 4, 0), second)
+    return jnp.where(low, first, pltpu.roll(second, 4, 0))
+
+
+def kernel(sizes, tokens, routes, gates, w_gate, w_up, w_down, out, *scratch):
+    (block, x, weight, gbuf, ubuf, dbuf, gate_acc, up_acc, hidden,
+     send_a, recv_a, keep_a, send_b, recv_b, keep_b, send_c, recv_c, keep_c, folded,
+     g_sem, u_sem, d_sem, zs, zr, ys, yr, cs, cr, as_, ar, bs, br, ts, tr) = scratch
+    width, hid, chunks = sizes
+    quarter = width // FOLD
+    k_rows = width // K_CHUNKS
+    per_quarter = K_CHUNKS // FOLD
+    piece = CHUNK // FOLD
+    part = lax.axis_index("parts")
+    me = lax.axis_index("tensor")
+    z, y, c = me // 4, me // 2 % 2, me % 2
+
+    def index(zz, yy, cc):
+        return zz * 4 + yy * 2 + cc
+
+    def z_of(k):
+        return (z + k) % 4
+
+    y_peer = index(z, 1 - y, c)
+    c_peer = index(z, y, 1 - c)
+
+    def gu_copy(step):
+        slot = step % GU_SLOTS
+        rows = pl.ds(pl.multiple_of(step * k_rows, k_rows), k_rows)
+        return (pltpu.make_async_copy(w_gate.at[rows, :], gbuf.at[slot], g_sem.at[slot]),
+                pltpu.make_async_copy(w_up.at[rows, :], ubuf.at[slot], u_sem.at[slot]))
+
+    def d_copy(step):
+        columns = pl.ds(pl.multiple_of(step * CHUNK, CHUNK), CHUNK)
+        return pltpu.make_async_copy(w_down.at[:, columns], dbuf.at[step], d_sem.at[step])
+
+    for step in range(GU_SLOTS):
+        for copy in gu_copy(step):
+            copy.start()
+
+    barrier = pltpu.get_barrier_semaphore()
+    for peer in [index(z_of(k), y, c) for k in (1, 2, 3)] + [y_peer, c_peer]:
+        pl.semaphore_signal(barrier, inc=1, device_id=(part, peer), device_id_type=MESH)
+
+    rows = tokens[...].astype(jnp.float32)
+    block[me, :, :quarter] = jnp.concatenate(
+        [rows[:, q * quarter:(q + 1) * quarter] for q in range(FOLD)], axis=0
+    ).astype(jnp.bfloat16)
+    ids = routes[...]
+    values = gates[...].astype(jnp.float32)
+    weights = []
+    for e in range(EXPERTS):
+        column = jnp.sum(jnp.where(ids == e, values, 0.0), axis=1, keepdims=True)
+        weights.append(jnp.broadcast_to(column, (ROWS_DEV, LANES)))
+    block[me, :, quarter:] = jnp.concatenate(weights, axis=0).astype(jnp.bfloat16)
+
+    pl.semaphore_wait(barrier, 5)
+
+    def send(source, target, s_sem, r_sem, peer):
+        return pltpu.make_async_remote_copy(
+            src_ref=source, dst_ref=target, send_sem=s_sem, recv_sem=r_sem,
+            device_id=(part, peer), device_id_type=MESH)
+
+    def z_send(k):
+        return send(block.at[me], block.at[me], zs.at[k], zr.at[k], index(z_of(k), y, c))
+
+    def y_send(k):
+        own = block.at[index(z_of(4 - k), y, c)]
+        return send(own, own, ys.at[k], yr.at[k], y_peer)
+
+    def c_send(dy, k):
+        own = block.at[index(z_of(4 - k), (y + dy) % 2, c)]
+        return send(own, own, cs.at[dy * 4 + k], cr.at[dy * 4 + k], c_peer)
+
+    def assemble(dy, dc):
+        base = dc * 32 + dy * 16
+        parts = [block[index(z_of(k), (y + dy) % 2, (c + dc) % 2)].astype(jnp.float32)
+                 for k in range(4)]
+        chosen = jnp.zeros((16, LANES), jnp.float32)
+        for q in range(FOLD):
+            tile = slice(q // 2 * 8, q // 2 * 8 + 8)
+            pairs = [spread(parts[2 * m][tile], parts[2 * m + 1][tile], q % 2) for m in (0, 1)]
+            both = jnp.concatenate(pairs, axis=0)
+            for h in range(per_quarter):
+                x[q * per_quarter + h, base:base + 16, :] = both[
+                    :, h * k_rows:(h + 1) * k_rows].astype(jnp.bfloat16)
+            chosen = jnp.where(z == q, both[:, quarter:], chosen)
+        weight[base:base + 16, :] = chosen
+
+    for k in (2, 3, 1):
+        z_send(k).start()
+    y_send(0).start()
+    c_send(0, 0).start()
+    y_send(0).wait_recv()
+    c_send(1, 0).start()
+    for k in (1, 3, 2):
+        z_send(k).wait_recv()
+        y_send(k).start()
+        c_send(0, k).start()
+    for step in range(min(D_EARLY, chunks)):
+        d_copy(step).start()
+    gate_acc[...] = jnp.zeros_like(gate_acc)
+    up_acc[...] = jnp.zeros_like(up_acc)
+    assemble(0, 0)
+    for k in (1, 3, 2):
+        y_send(k).wait_recv()
+        c_send(1, k).start()
+    assemble(1, 0)
+    for k in range(4):
+        c_send(0, k).wait_recv()
+    assemble(0, 1)
+    for k in range(4):
+        c_send(1, k).wait_recv()
+    assemble(1, 1)
+
+    tile_n = min(512, hid)
+
+    def gate_up(step, carry):
+        slot = step % GU_SLOTS
+        lhs = x[step]
+        for copy, buffer, total in zip(gu_copy(step), (gbuf, ubuf), (gate_acc, up_acc)):
+            copy.wait()
+            for n in range(hid // tile_n):
+                columns = slice(n * tile_n, (n + 1) * tile_n)
+                total[:, columns] += jnp.dot(
+                    lhs, buffer[slot, :, columns], preferred_element_type=jnp.float32)
+
+        @pl.when(step + GU_SLOTS < K_CHUNKS)
+        def _():
+            for copy in gu_copy(step + GU_SLOTS):
+                copy.start()
+
+        late = -(-(chunks - D_EARLY) // (K_CHUNKS - GU_SLOTS))
+        for i in range(max(late, 0)):
+            number = D_EARLY + (step - GU_SLOTS) * late + i
+
+            @pl.when((step >= GU_SLOTS) & (number < chunks))
+            def _():
+                d_copy(number).start()
+
+        return carry
+
+    lax.fori_loop(0, K_CHUNKS, gate_up, 0)
+    for n in range(hid // tile_n):
+        columns = slice(n * tile_n, (n + 1) * tile_n)
+        gate = gate_acc[:, columns]
+        hidden[:, columns] = (gate / (1.0 + jnp.exp(-gate)) * up_acc[:, columns]).astype(jnp.bfloat16)
+
+    def a_send(n):
+        return send(send_a.at[n], recv_a.at[n], as_.at[n], ar.at[n], c_peer)
+
+    def b_send(n):
+        return send(send_b.at[n], recv_b.at[n], bs.at[n], br.at[n], y_peer)
+
+    def t_send(n, k):
+        return send(send_c.at[n, k - 1], recv_c.at[n, k - 1], ts.at[n, k - 1], tr.at[n, k - 1],
+                    index(z_of(k), y, c))
+
+    def down(step, carry):
+        n_d = step - 3 * SKEW
+
+        @pl.when(n_d >= 0)
+        def _():
+            for k in (1, 2, 3):
+                t_send(n_d, k).wait_recv()
+            folded[n_d] = keep_c[n_d] + (
+                recv_c[n_d, 0].astype(jnp.float32) + recv_c[n_d, 1].astype(jnp.float32)
+                + recv_c[n_d, 2].astype(jnp.float32))
+
+        n_c = step - 2 * SKEW
+
+        @pl.when((n_c >= 0) & (n_c < chunks))
+        def _():
+            b_send(n_c).wait_recv()
+            total = keep_b[n_c] + recv_b[n_c].astype(jnp.float32)
+            for k in (2, 1, 3, 0):
+                half = total[k // 2 * 8:k // 2 * 8 + 8]
+                both = jnp.concatenate(
+                    [spread(half[:, 2 * m * piece:(2 * m + 1) * piece],
+                            half[:, (2 * m + 1) * piece:(2 * m + 2) * piece], k % 2)
+                     for m in (0, 1)], axis=0)
+                if k == 0:
+                    keep_c[n_c] = both
+                else:
+                    send_c[n_c, k - 1] = both.astype(jnp.bfloat16)
+                    t_send(n_c, k).start()
+
+        n_b = step - SKEW
+
+        @pl.when((n_b >= 0) & (n_b < chunks))
+        def _():
+            a_send(n_b).wait_recv()
+            send_b[n_b] = (keep_a[n_b, 16:, :] + recv_a[n_b, 16:, :].astype(jnp.float32)).astype(jnp.bfloat16)
+            b_send(n_b).start()
+            keep_b[n_b] = keep_a[n_b, :16, :] + recv_a[n_b, :16, :].astype(jnp.float32)
+
+        @pl.when(step < chunks)
+        def _():
+            d_copy(step).wait()
+            scale = weight[...]
+            product = jnp.dot(hidden[...], dbuf[step], preferred_element_type=jnp.float32)
+            product = product * jnp.concatenate([scale] * (CHUNK // LANES), axis=1)
+            send_a[step] = product[32:].astype(jnp.bfloat16)
+            a_send(step).start()
+            keep_a[step] = product[:32]
+
+        return carry
+
+    lax.fori_loop(0, chunks + 3 * SKEW, down, 0)
+
+    for n in range(chunks):
+        pieces = []
+        for j in range(FOLD):
+            half = folded[n, j // 2 * 8:j // 2 * 8 + 8, :]
+            pieces.append(pltpu.roll(half, 4, 0) if j % 2 else half)
+        whole = jnp.concatenate(pieces, axis=1)
+        out[:, n * CHUNK:(n + 1) * CHUNK] = whole[:ROWS_DEV].astype(jnp.bfloat16)
+
+    for k in (1, 2, 3):
+        z_send(k).wait_send()
+    for k in range(4):
+        y_send(k).wait_send()
+        c_send(0, k).wait_send()
+        c_send(1, k).wait_send()
+
+    def drain(n, carry):
+        a_send(n).wait_send()
+        b_send(n).wait_send()
+        for k in (1, 2, 3):
+            t_send(n, k).wait_send()
+        return carry
+
+    lax.fori_loop(0, chunks, drain, 0)
+
+
+def fused(tokens, route_ids, gate_values, w_gate, w_up, w_down):
+    width = tokens.shape[1]
+    hid = w_gate.shape[1]
+    chunks = width // CHUNK
+    quarter = width // FOLD
+    k_rows = width // K_CHUNKS
+    piece = CHUNK // FOLD
+    rows = DEVICES * ROWS_DEV
+    bf16, f32, dma = jnp.bfloat16, jnp.float32, pltpu.SemaphoreType.DMA
+    scratch = [
+        pltpu.VMEM((DEVICES, 16, quarter + LANES), bf16),
+        pltpu.VMEM((K_CHUNKS, rows, k_rows), bf16),
+        pltpu.VMEM((rows, LANES), f32),
+        pltpu.VMEM((GU_SLOTS, k_rows, hid), bf16),
+        pltpu.VMEM((GU_SLOTS, k_rows, hid), bf16),
+        pltpu.VMEM((chunks, hid, CHUNK), bf16),
+        pltpu.VMEM((rows, hid), f32),
+        pltpu.VMEM((rows, hid), f32),
+        pltpu.VMEM((rows, hid), bf16),
+        pltpu.VMEM((chunks, 32, CHUNK), bf16),
+        pltpu.VMEM((chunks, 32, CHUNK), bf16),
+        pltpu.VMEM((chunks, 32, CHUNK), f32),
+        pltpu.VMEM((chunks, 16, CHUNK), bf16),
+        pltpu.VMEM((chunks, 16, CHUNK), bf16),
+        pltpu.VMEM((chunks, 16, CHUNK), f32),
+        pltpu.VMEM((chunks, 3, 16, piece), bf16),
+        pltpu.VMEM((chunks, 3, 16, piece), bf16),
+        pltpu.VMEM((chunks, 16, piece), f32),
+        pltpu.VMEM((chunks, 16, piece), f32),
+        dma((GU_SLOTS,)), dma((GU_SLOTS,)), dma((chunks,)),
+        dma((4,)), dma((4,)), dma((4,)), dma((4,)), dma((8,)), dma((8,)),
+        dma((chunks,)), dma((chunks,)), dma((chunks,)), dma((chunks,)),
+        dma((chunks, 3)), dma((chunks, 3)),
+    ]
+    vmem = pl.BlockSpec(memory_space=pltpu.VMEM)
+    hbm = pl.BlockSpec(memory_space=pl.ANY)
+    return pl.pallas_call(
+        functools.partial(kernel, (width, hid, chunks)),
+        out_shape=jax.ShapeDtypeStruct((ROWS_DEV, width), bf16),
+        in_specs=[vmem, vmem, vmem, hbm, hbm, hbm],
+        out_specs=vmem,
+        scratch_shapes=scratch,
+        compiler_params=pltpu.CompilerParams(
+            collective_id=0, has_side_effects=True, vmem_limit_bytes=60 * 2**20),
+        cost_estimate=pl.CostEstimate(
+            flops=6 * rows * width * hid, bytes_accessed=6 * width * hid, transcendentals=rows * hid),
+    )(tokens, route_ids, gate_values, w_gate, w_up, w_down)
 
 
 def partner(shard, axis, stride):
@@ -124,6 +425,17 @@
         P("tensor", None),
     )
     out_specs = P(("parts", "tensor"), None)
-    return jax.shard_map(
-        per_device, mesh=mesh, in_specs=in_specs, out_specs=out_specs, check_vma=False
-    )
+    rows = ROWS_DEV * DEVICES
+
+    def whole(tokens, route_ids, gate_values, w_gate, w_up, w_down):
+        width, hid = w_gate.shape[0], w_gate.shape[1] // mesh.shape["tensor"]
+        fits = mesh.shape["tensor"] == DEVICES and tokens.shape[0] == rows * mesh.shape["parts"]
+        fits = fits and width % (K_CHUNKS * LANES) == 0 and hid % 512 == 0
+        fits = fits and width * hid <= 6144 * 2048
+        return shard(fused if fits else per_device)(
+            tokens, route_ids, gate_values, w_gate, w_up, w_down)
+
+    shard = lambda body: jax.shard_map(
+        body, mesh=mesh, in_specs=in_specs, out_specs=out_specs, check_vma=False
+    )
+    return whole

time: 114 us -> 60.4 us (0.53)
  Pallas kernels: 0 us -> 56 us
  matrix products: 31.6 us -> 0 us
  blocking collectives: 29.2 us -> 0 us
  waiting for transfers between devices: 18.9 us -> 0 us
  starting transfers between devices: 15.3 us -> 0 us
  local copies, waits for them, and re-layouts: 13.4 us -> 4.09 us
  other arithmetic: 4.3 us -> 0 us
    pallas_call x0 -> x1, Pallas kernels: none -> 56 us  [fused(): pl.pallas_call(functools.partial(kernel, (width, hid, chunks)), out_shape...]
    dot_general x2 -> x0, matrix products: 31.6 us -> none  [the longest x1 18.4 us: block_work(): output_rows = jnp.dot(hidden, w_down, preferred_element_type=jnp.float32)]
    all_gather x1 -> x0, blocking collectives: 29.2 us -> none  [per_device(): all_routes = lax.all_gather(route_ids, 'tensor', axis=0, tiled=True)]
    ppermute x5 -> x0, waiting for transfers between devices: 18.9 us -> none  [the longest x2 14.1 us: partner(): lax.ppermute(shard, axis, [(i, i ^ 1 << stride) for i in range(lax.axis_s...]
    gather x9 -> x0, local copies, waits for them, and re-layouts: 8.22 us -> none  [the longest x2 3.5 us: per_device(): jnp.take(partial_value, landing.reshape(-1), axis=0, mode='fill', fill_va...]
    ppermute x5 -> x0, starting transfers between devices: 7.93 us -> none  [the longest x3 5.99 us: from_behind(): return lax.ppermute(block, axis, route)]
    all_to_all x1 -> x0, starting transfers between devices: 7.39 us -> none  [per_device(): lax.all_to_all(outgoing, 'tensor', split_axis=0, concat_axis=0, tiled=True)]
    unnamed x8 -> x3, local copies, waits for them, and re-layouts: 0.02 us -> 4.09 us
  transfers between devices with their start and end apart: 6 -> 0, of which waited for: 4 -> 0; matrix products, arithmetic and copies ran while one was open for 3% -> 0% of each run, Pallas kernels for 0% -> 0%
where the time goes in v1:
time: 60.4 us; the launch traced here: 60.1 us
  Pallas kernels  56 us (93%)
  local copies, waits for them, and re-layouts  4.09 us (7%)
    pallas_call x1, Pallas kernels, fused(): pl.pallas_call(functools.partial(kernel, (width, hid, chunks)), out_shape...  56 us
    unnamed x3, local copies, waits for them, and re-layouts  4.09 us

profile of v1, /device:TPU:0, one launch (start us, length us, event | category | flops | bytes accessed | tf_op | source)
XLA Modules:
  0.0 60.1 jit_solution(4240961651206329050)
XLA Ops:
  0.0 1.3 %copy.8.gates = bf16[4,2]{1,0:T(4,128)(2,1)} copy(bf16[4,2]{0,1:T(2,128)(2,1)} %param.8) | data formatting | bytes 32 | tf_op args[2]
  1.3 1.3 %copy.7.routes = s32[4,2]{1,0:T(4,128)} copy(s32[4,2]{0,1:T(2,128)} %param.7) | data formatting | bytes 64 | tf_op args[1]
  2.7 56.0 %shard_map.64 = bf16[4,6144]{1,0:T(4,128)(2,1)} custom-call(bf16[4,6144]{1,0:T(4,128)(2,1)} %tokens.1, s32[4,2]{1,0:T(4,128)} %copy.7.routes, bf16[4,2]{1,0:T(4,128)(2,1)} %copy.8.gates, bf16[6144,2048]{1,0:T(8,128)(2,1)} %w_gate.1, bf16[6144,2048]{1,0:T(8,128)(2,1)} %w_up.1, bf16[2048,6144]{1,0:T(8,128)(2,1)} %w_down.1), custom_call_target="tpu_custom_call" | custom-call | flops 4831838208 | bytes 75497472 | tf_op jit(solution)/shard_map/pallas_call | solution.py:299
  58.7 1.4 %copy.10 = bf16[4,6144]{1,0:T(4,128)(2,1)} copy(bf16[4,6144]{1,0:T(4,128)(2,1)} %shard_map.64) | data formatting | bytes 98304

commit v2 on v1

--- a/solution.py
+++ b/solution.py
@@ -15,9 +15,9 @@
 FOLD = 4
 K_CHUNKS = 8
 GU_SLOTS = 4
-D_EARLY = 4
+D_EARLY = 8
 CHUNK = 512
-SKEW = 2
+SKEW = 12
 LANES = 128
 MESH = pl.DeviceIdType.MESH
 
@@ -29,7 +29,7 @@
     return jnp.where(low, first, pltpu.roll(second, 4, 0))
 
 
-def kernel(sizes, tokens, routes, gates, w_gate, w_up, w_down, out, *scratch):
+def kernel(sizes, tokens, by_expert, w_gate, w_up, w_down, out, *scratch):
     (block, x, weight, gbuf, ubuf, dbuf, gate_acc, up_acc, hidden,
      send_a, recv_a, keep_a, send_b, recv_b, keep_b, send_c, recv_c, keep_c, folded,
      g_sem, u_sem, d_sem, zs, zr, ys, yr, cs, cr, as_, ar, bs, br, ts, tr) = scratch
@@ -73,13 +73,8 @@
     block[me, :, :quarter] = jnp.concatenate(
         [rows[:, q * quarter:(q + 1) * quarter] for q in range(FOLD)], axis=0
     ).astype(jnp.bfloat16)
-    ids = routes[...]
-    values = gates[...].astype(jnp.float32)
-    weights = []
-    for e in range(EXPERTS):
-        column = jnp.sum(jnp.where(ids == e, values, 0.0), axis=1, keepdims=True)
-        weights.append(jnp.broadcast_to(column, (ROWS_DEV, LANES)))
-    block[me, :, quarter:] = jnp.concatenate(weights, axis=0).astype(jnp.bfloat16)
+    block[me, :, quarter:] = jnp.concatenate(
+        [by_expert[e] for e in range(EXPERTS)], axis=0).astype(jnp.bfloat16)
 
     pl.semaphore_wait(barrier, 5)
 
@@ -294,19 +289,22 @@
         dma((chunks,)), dma((chunks,)), dma((chunks,)), dma((chunks,)),
         dma((chunks, 3)), dma((chunks, 3)),
     ]
+    chosen = route_ids[None, :, :] == jnp.arange(EXPERTS, dtype=jnp.int32)[:, None, None]
+    by_expert = jnp.sum(jnp.where(chosen, gate_values.astype(f32)[None], 0.0), axis=2)
+    by_expert = jnp.broadcast_to(by_expert[:, :, None], (EXPERTS, ROWS_DEV, LANES))
     vmem = pl.BlockSpec(memory_space=pltpu.VMEM)
     hbm = pl.BlockSpec(memory_space=pl.ANY)
     return pl.pallas_call(
         functools.partial(kernel, (width, hid, chunks)),
         out_shape=jax.ShapeDtypeStruct((ROWS_DEV, width), bf16),
-        in_specs=[vmem, vmem, vmem, hbm, hbm, hbm],
+        in_specs=[vmem, vmem, hbm, hbm, hbm],
         out_specs=vmem,
         scratch_shapes=scratch,
         compiler_params=pltpu.CompilerParams(
             collective_id=0, has_side_effects=True, vmem_limit_bytes=60 * 2**20),
         cost_estimate=pl.CostEstimate(
             flops=6 * rows * width * hid, bytes_accessed=6 * width * hid, transcendentals=rows * hid),
-    )(tokens, route_ids, gate_values, w_gate, w_up, w_down)
+    )(tokens, by_expert, w_gate, w_up, w_down)
 
 
 def partner(shard, axis, stride):

time: 60.4 us -> 48.3 us (0.80)
  Pallas kernels: 56 us -> 44.5 us
  local copies, waits for them, and re-layouts: 4.09 us -> 2.11 us
  other arithmetic: 0 us -> 1.35 us
    pallas_call x1, Pallas kernels: 56 us -> 44.5 us  [fused(): pl.pallas_call(functools.partial(kernel, (width, hid, chunks)), out_shape...]
    unnamed x3 -> x1, local copies, waits for them, and re-layouts: 4.09 us -> 1.44 us
    reduce_sum x0 -> x1, other arithmetic: none -> 0.69 us  [fused(): jnp.sum(jnp.where(chosen, gate_values.astype(f32)[None], 0.0), axis=2)]
    broadcast_in_dim x0 -> x1, local copies, waits for them, and re-layouts: none -> 0.67 us  [fused(): jnp.broadcast_to(by_expert[:, :, None], (EXPERTS, ROWS_DEV, LANES))]
    convert_element_type x0 -> x1, other arithmetic: none -> 0.66 us  [fused(): gate_values.astype(f32)[None]]
where the time goes in v2:
time: 48.3 us; the launch traced here: 48 us
  Pallas kernels  44.5 us (92%)
  local copies, waits for them, and re-layouts  2.11 us (4%)
  other arithmetic  1.35 us (3%)
    pallas_call x1, Pallas kernels, fused(): pl.pallas_call(functools.partial(kernel, (width, hid, chunks)), out_shape...  44.5 us
    unnamed x1, local copies, waits for them, and re-layouts  1.44 us

profile of v2, /device:TPU:0, one launch (start us, length us, event | category | flops | bytes accessed | tf_op | source)
XLA Modules:
  0.0 48.0 jit_solution(5251570092868425267)
XLA Ops:
  0.0 0.7 %convert_element_type.3 = f32[4,2]{0,1:T(2,128)S(1)} convert(bf16[4,2]{0,1:T(2,128)(2,1)} %param.8) | non-fusion elementwise | flops 8 | bytes 48 | tf_op jit(solution)/shard_map/convert_element_type | solution.py:293
  0.7 0.7 %select_reduce_fusion = f32[4,4]{1,0:T(4,128)S(1)} fusion(f32[4,2]{0,1:T(2,128)S(1)} %convert_element_type.3, s32[4,2]{0,1:T(2,128)} %param.7), kind=kLoop, calls=%fused_computation | loop fusion | flops 80 | bytes 128 | tf_op jit(solution)/shard_map/reduce_sum | solution.py:293
  1.4 0.7 %broadcast_in_dim.23.by_expert = f32[4,4,128]{2,1,0:T(4,128)} broadcast(f32[4,4]{1,0:T(4,128)S(1)} %select_reduce_fusion), dimensions={0,1} | broadcast | bytes 8256 | tf_op jit(solution)/shard_map/broadcast_in_dim | solution.py:294
  2.0 44.5 %shard_map.64 = bf16[4,6144]{1,0:T(4,128)(2,1)} custom-call(bf16[4,6144]{1,0:T(4,128)(2,1)} %tokens.1, f32[4,4,128]{2,1,0:T(4,128)} %broadcast_in_dim.23.by_expert, bf16[6144,2048]{1,0:T(8,128)(2,1)} %w_gate.1, bf16[6144,2048]{1,0:T(8,128)(2,1)} %w_up.1, bf16[2048,6144]{1,0:T(8,128)(2,1)} %w_down.1), custom_call_target="tpu_custom_call" | custom-call | flops 4831838208 | bytes 75497472 | tf_op jit(solution)/shard_map/pallas_call | solution.py:297
  46.6 1.4 %copy.10 = bf16[4,6144]{1,0:T(4,128)(2,1)} copy(bf16[4,6144]{1,0:T(4,128)(2,1)} %shard_map.64) | data formatting | bytes 98304
